TPU v7x, 32 devices: a whole 2x2x4 slice. The times are simulated.
32 devices in a mesh: grp: 8 (over z, y), blk: 4 (over x, core).
Axes of the slice: x: 2, y: 2, z: 4, core: 2. Of those that a mesh axis runs over, the one named last changes fastest.
Arguments:
- src_codes: int32 [32768, 1024], P(('grp', 'blk')), may hold values from -119 to 119
- src_exps: int32 [32768, 8], P(('grp', 'blk')), may hold values from 0 to 3
- signs: int32 [32768, 256], P(('grp', 'blk')), may hold values from 0 to 1
- tgt_codes: int32 [1024, 1024], P('blk'), may hold values from -119 to 119
- tgt_exps: int32 [1024, 8], P('blk'), may hold values from 0 to 3
Outputs:
- kernel_product: float32 [1024, 256], P('blk', 'grp')
All inputs are finite; a program needn't handle non-finite values.
Results may differ from a plain program's by a relative error of at most 0.003.
Values may be sent and summed in bfloat16 or wider, within the bound.
A program may use at most 64 MiB of HBM per device.

v0:
```python
import math

import jax
import jax.numpy as jnp
from jax import lax
from jax.sharding import PartitionSpec as P

kernel_rate = 20.0


def shifted(block, axis, distance):
    devices = range(lax.axis_size(axis))
    route = [((i - distance) % len(devices), i) for i in devices]
    return lax.ppermute(block, axis, route)


def dequantize(codes, exponents):
    points, columns = codes.shape
    blocks = exponents.shape[1]
    factor = jnp.zeros(exponents.shape, jnp.float32)
    for level_index in range(4):
        factor = factor + jnp.where(exponents == level_index, 2.0 ** (level_index - 9), 0.0)
    scaled_codes = (
        codes.reshape(points, blocks, columns // blocks).astype(jnp.float32) * factor[:, :, None]
    )
    return scaled_codes.reshape(points, columns).astype(jnp.bfloat16)


def squares(points_bf):
    widened = points_bf.astype(jnp.float32)
    return jnp.sum(widened * widened, axis=1)


def kernel_block(targets_bf, sources_bf, source_sq, rhs_values):
    target_sq = squares(targets_bf)
    inner_products = lax.dot_general(
        targets_bf, sources_bf, (((1,), (1,)), ((), ())), preferred_element_type=jnp.float32
    )
    squared = target_sq[:, None] + source_sq[None, :] - 2.0 * inner_products
    scaled = kernel_rate * jnp.sqrt(squared) / math.sqrt(targets_bf.shape[1])
    matern = ((1.0 + scaled + scaled * scaled / 3.0) * jnp.exp(-scaled)).astype(jnp.bfloat16)
    return jnp.dot(matern, rhs_values, preferred_element_type=jnp.float32)


def per_device(src_codes, src_exps, signs, tgt_codes, tgt_exps):
    sources_bf = dequantize(src_codes, src_exps)
    targets_bf = dequantize(tgt_codes, tgt_exps)
    rhs_values = (2 * signs - 1).astype(jnp.bfloat16)
    source_sq = squares(sources_bf)
    cycle_size = lax.axis_size("blk")
    group_size = lax.axis_size("grp")
    block_rows = targets_bf.shape[0]
    rhs_count = rhs_values.shape[1]

    def contribution(points_bf):
        return kernel_block(points_bf, sources_bf, source_sq, rhs_values)

    halfway = block_rows // 2

    def advance(counter, carried):
        ahead_bf, ahead_sums, behind_bf, behind_sums = carried
        ahead_sums = ahead_sums + contribution(ahead_bf)
        behind_sums = behind_sums + contribution(behind_bf)
        ahead_bf = shifted(ahead_bf, "blk", 1)
        ahead_sums = shifted(ahead_sums, "blk", 1)
        behind_bf = shifted(behind_bf, "blk", -1)
        behind_sums = shifted(behind_sums, "blk", -1)
        return (ahead_bf, ahead_sums, behind_bf, behind_sums)

    start_sums = jnp.zeros((halfway, rhs_count), jnp.float32)
    carried = (targets_bf[:halfway], start_sums, targets_bf[halfway:], start_sums)
    ahead_bf, ahead_sums, behind_bf, behind_sums = lax.fori_loop(
        0, cycle_size - 1, advance, carried
    )
    ahead_sums = shifted(ahead_sums + contribution(ahead_bf), "blk", 1)
    behind_sums = shifted(behind_sums + contribution(behind_bf), "blk", -1)
    gathered_sums = jnp.concatenate([ahead_sums, behind_sums], axis=0)
    owned_sums = lax.psum_scatter(gathered_sums, "grp", scatter_dimension=1, tiled=True)
    source_total = src_codes.shape[0] * group_size * cycle_size
    return owned_sums * (4.0 / math.sqrt(source_total))


def solution(mesh):
    placed = (
        P(("grp", "blk"), None),
        P(("grp", "blk"), None),
        P(("grp", "blk"), None),
        P("blk", None),
        P("blk", None),
    )
    return jax.shard_map(
        per_device, mesh=mesh, in_specs=placed, out_specs=P("blk", "grp"), check_vma=False
    )
```

profile of v0, /device:TPU:0, one launch (start us, length us, event | category | flops | bytes accessed | tf_op | source)
XLA Modules:
  0.0 129.6 jit_solution(16532590065928404530)
XLA Ops:
  6.5 0.9 select_add_fusion
  7.6 2.1 %add_convert_fusion = bf16[1024,256]{1,0:T(8,128)(2,1)} fusion(s32[1024,256]{1,0:T(8,128)} %param.9), kind=kLoop, calls=%fused_computation.51 | loop fusion | flops 786432 | bytes 1572864 | tf_op jit(solution)/shard_map/convert_element_type | solution.py:48
  9.9 0.3 mul.121
  10.2 0.3 fusion.35
  10.6 1.1 mul.124
  11.8 1.0 copy-done
  12.8 0.9 multiply_reduce_fusion.2
  13.7 34.4 %while.19 = (s32[]{:T(128)}, bf16[128,1024]{1,0:T(8,128)(2,1)S(1)}, f32[128,256]{1,0:T(8,128)S(1)}, bf16[128,1024]{1,0:T(8,128)(2,1)S(1)}, f32[128,256]{1,0:T(8,...) while((s32[]{:T(128)}, bf16[128,1024]{1,0:T(8,128)(2,1)S(1)}, ...), condition=%wide.region_4.5_spmd, body=%wide.region_1.4_spmd.sunk | while | flops 674823936 | bytes 11020541 | solution.py:72
  13.8 0.5 collective-permute-start
  14.4 2.1 %convolution_add_fusion.6 = f32[128,256]{1,0:T(8,128)S(1)} fusion(f32[128,256]{1,0:T(8,128)S(1)} %get-tuple-element.215, bf16[1024,256]{1,0:T(8,128)(2,1)} %get-tuple-element.229, bf16[128,1024]{1,0:T(8,128)(2,1)S(1)} %copy.28, bf16[1024,1024]{1,0:T(8,128)(2,1)S(1)} %get-tuple-element.228, f32[1024]{0:T(1024)S(1)} %get-tuple-element.227, ...), kind=kOutput, calls=%fused_computation.9.clone.1 | convolution fusion | flops 337018880 | bytes 3150336 | tf_op jit(solution)/shard_map/while/body/eval_jaxpr/dot_general | solution.py:42
  16.5 2.7 %collective-permute-start.1 = (f32[128,256]{1,0:T(8,128)S(1)}, f32[128,256]{1,0:T(8,128)S(1)}, u32[]{:S(2)}, u32[]{:S(2)}) collective-permute-start(f32[128,256]{1,0:T(8,128)S(1)} %convolution_add_fusion.6), channel_id=1, source_target_pairs={{3,0},{0,1},{1,2},{2,3},{7,4},{4,5},{5,6},{6,7},{11,8},{8,9},{9,10... | collective-permute-start | bytes 393224 | tf_op jit(solution)/shard_map/while/body/eval_jaxpr/ppermute | solution.py:14
  19.4 2.8 %convolution_add_fusion.7 = f32[128,256]{1,0:T(8,128)} fusion(f32[128,256]{1,0:T(8,128)S(1)} %get-tuple-element.217, bf16[1024,256]{1,0:T(8,128)(2,1)} %get-tuple-element.229, bf16[128,1024]{1,0:T(8,128)(2,1)S(1)} %copy.30, bf16[1024,1024]{1,0:T(8,128)(2,1)S(1)} %get-tuple-element.228, f32[128]{0:T(128)S(1)} %multiply_reduce_fusion.8, ...), kind=kOutput, calls=%fused_computation.8.clone.1 | convolution fusion | flops 337018880 | bytes 3150336 | tf_op jit(solution)/shard_map/while/body/eval_jaxpr/dot_general | solution.py:42
  22.2 3.6 %collective-permute-done.3 = f32[128,256]{1,0:T(8,128)S(1)} collective-permute-done((f32[128,256]{1,0:T(8,128)}, f32[128,256]{1,0:T(8,128)S(1)}, u32[]{:S(2)}, u32[]{:S(2)}) %collective-permute-start.3) | collective-permute-done | bytes 131104 | tf_op jit(solution)/shard_map/while/body/eval_jaxpr/ppermute | solution.py:14
  25.8 1.5 %collective-permute-start = (bf16[128,1024]{1,0:T(8,128)(2,1)S(1)}, bf16[128,1024]{1,0:T(8,128)(2,1)S(1)}, u32[]{:S(2)}, u32[]{:S(2)}) collective-permute-start(bf16[128,1024]{1,0:T(8,128)(2,1)S(1)} %copy.28), channel_id=1, source_target_pairs={{3,0},{0,1},{1,2},{2,3},{7,4},{4,5},{5,6},{6,7},{11,8},{8,9},{9,10... | collective-permute-start | bytes 786440 | tf_op jit(solution)/shard_map/while/body/eval_jaxpr/ppermute | solution.py:14
  27.5 2.1 %convolution_add_fusion.6 = f32[128,256]{1,0:T(8,128)S(1)} fusion(f32[128,256]{1,0:T(8,128)S(1)} %get-tuple-element.215, bf16[1024,256]{1,0:T(8,128)(2,1)} %get-tuple-element.229, bf16[128,1024]{1,0:T(8,128)(2,1)S(1)} %copy.28, bf16[1024,1024]{1,0:T(8,128)(2,1)S(1)} %get-tuple-element.228, f32[1024]{0:T(1024)S(1)} %get-tuple-element.227, ...), kind=kOutput, calls=%fused_computation.9.clone.1 | convolution fusion | flops 337018880 | bytes 3150336 | tf_op jit(solution)/shard_map/while/body/eval_jaxpr/dot_general | solution.py:42
  29.7 1.8 %collective-permute-start.2 = (bf16[128,1024]{1,0:T(8,128)(2,1)S(1)}, bf16[128,1024]{1,0:T(8,128)(2,1)S(1)}, u32[]{:S(2)}, u32[]{:S(2)}) collective-permute-start(bf16[128,1024]{1,0:T(8,128)(2,1)S(1)} %copy.30), channel_id=1, source_target_pairs={{1,0},{2,1},{3,2},{0,3},{5,4},{6,5},{7,6},{4,7},{9,8},{10,9},{11,1... | collective-permute-start | bytes 786440 | tf_op jit(solution)/shard_map/while/body/eval_jaxpr/ppermute | solution.py:14
  31.6 2.8 %convolution_add_fusion.7 = f32[128,256]{1,0:T(8,128)} fusion(f32[128,256]{1,0:T(8,128)S(1)} %get-tuple-element.217, bf16[1024,256]{1,0:T(8,128)(2,1)} %get-tuple-element.229, bf16[128,1024]{1,0:T(8,128)(2,1)S(1)} %copy.30, bf16[1024,1024]{1,0:T(8,128)(2,1)S(1)} %get-tuple-element.228, f32[128]{0:T(128)S(1)} %multiply_reduce_fusion.8, ...), kind=kOutput, calls=%fused_computation.8.clone.1 | convolution fusion | flops 337018880 | bytes 3150336 | tf_op jit(solution)/shard_map/while/body/eval_jaxpr/dot_general | solution.py:42
  34.4 2.8 %collective-permute-done.3 = f32[128,256]{1,0:T(8,128)S(1)} collective-permute-done((f32[128,256]{1,0:T(8,128)}, f32[128,256]{1,0:T(8,128)S(1)}, u32[]{:S(2)}, u32[]{:S(2)}) %collective-permute-start.3) | collective-permute-done | bytes 131104 | tf_op jit(solution)/shard_map/while/body/eval_jaxpr/ppermute | solution.py:14
  37.3 0.9 collective-permute-start
  38.3 2.1 %convolution_add_fusion.6 = f32[128,256]{1,0:T(8,128)S(1)} fusion(f32[128,256]{1,0:T(8,128)S(1)} %get-tuple-element.215, bf16[1024,256]{1,0:T(8,128)(2,1)} %get-tuple-element.229, bf16[128,1024]{1,0:T(8,128)(2,1)S(1)} %copy.28, bf16[1024,1024]{1,0:T(8,128)(2,1)S(1)} %get-tuple-element.228, f32[1024]{0:T(1024)S(1)} %get-tuple-element.227, ...), kind=kOutput, calls=%fused_computation.9.clone.1 | convolution fusion | flops 337018880 | bytes 3150336 | tf_op jit(solution)/shard_map/while/body/eval_jaxpr/dot_general | solution.py:42
  40.5 1.8 %collective-permute-start.2 = (bf16[128,1024]{1,0:T(8,128)(2,1)S(1)}, bf16[128,1024]{1,0:T(8,128)(2,1)S(1)}, u32[]{:S(2)}, u32[]{:S(2)}) collective-permute-start(bf16[128,1024]{1,0:T(8,128)(2,1)S(1)} %copy.30), channel_id=1, source_target_pairs={{1,0},{2,1},{3,2},{0,3},{5,4},{6,5},{7,6},{4,7},{9,8},{10,9},{11,1... | collective-permute-start | bytes 786440 | tf_op jit(solution)/shard_map/while/body/eval_jaxpr/ppermute | solution.py:14
  42.4 2.8 %convolution_add_fusion.7 = f32[128,256]{1,0:T(8,128)} fusion(f32[128,256]{1,0:T(8,128)S(1)} %get-tuple-element.217, bf16[1024,256]{1,0:T(8,128)(2,1)} %get-tuple-element.229, bf16[128,1024]{1,0:T(8,128)(2,1)S(1)} %copy.30, bf16[1024,1024]{1,0:T(8,128)(2,1)S(1)} %get-tuple-element.228, f32[128]{0:T(128)S(1)} %multiply_reduce_fusion.8, ...), kind=kOutput, calls=%fused_computation.8.clone.1 | convolution fusion | flops 337018880 | bytes 3150336 | tf_op jit(solution)/shard_map/while/body/eval_jaxpr/dot_general | solution.py:42
  45.2 2.8 %collective-permute-done.3 = f32[128,256]{1,0:T(8,128)S(1)} collective-permute-done((f32[128,256]{1,0:T(8,128)}, f32[128,256]{1,0:T(8,128)S(1)}, u32[]{:S(2)}, u32[]{:S(2)}) %collective-permute-start.3) | collective-permute-done | bytes 131104 | tf_op jit(solution)/shard_map/while/body/eval_jaxpr/ppermute | solution.py:14
  48.2 2.1 %convolution_add_fusion.3 = f32[128,256]{1,0:T(8,128)S(1)} fusion(f32[128,256]{1,0:T(8,128)S(1)} %get-tuple-element.131, bf16[1024,256]{1,0:T(8,128)(2,1)} %add_convert_fusion, bf16[128,1024]{1,0:T(8,128)(2,1)S(1)} %get-tuple-element.132, bf16[1024,1024]{1,0:T(8,128)(2,1)S(1)} %get-tuple-element.236, f32[1024]{0:T(1024)S(1)} %get-tuple-element.244, ...), kind=kOutput, calls=%fused_computation.48 | convolution fusion | flops 337018880 | bytes 3150336 | tf_op jit(solution)/shard_map/dot_general | solution.py:42
  50.3 1.5 %collective-permute-start.4 = (f32[128,256]{1,0:T(8,128)S(1)}, f32[128,256]{1,0:T(8,128)S(1)}, u32[]{:S(2)}, u32[]{:S(2)}) collective-permute-start(f32[128,256]{1,0:T(8,128)S(1)} %convolution_add_fusion.3), channel_id=1, source_target_pairs={{3,0},{0,1},{1,2},{2,3},{7,4},{4,5},{5,6},{6,7},{11,8},{8,9},{9,10... | collective-permute-start | bytes 393224 | tf_op jit(solution)/shard_map/ppermute | solution.py:14
  52.0 2.1 %convolution_add_fusion.2 = f32[128,256]{1,0:T(8,128)S(1)} fusion(f32[128,256]{1,0:T(8,128)S(1)} %get-tuple-element.133, bf16[1024,256]{1,0:T(8,128)(2,1)} %add_convert_fusion, bf16[128,1024]{1,0:T(8,128)(2,1)S(1)} %get-tuple-element.134, bf16[1024,1024]{1,0:T(8,128)(2,1)S(1)} %get-tuple-element.236, f32[128]{0:T(128)S(1)} %multiply_reduce_fusion.3, ...), kind=kOutput, calls=%fused_computation.47 | convolution fusion | flops 337018880 | bytes 3150336 | tf_op jit(solution)/shard_map/dot_general | solution.py:42
  54.1 0.4 collective-permute-start.5
  54.5 0.3 collective-permute-done.4
  54.8 2.2 %collective-permute-done.5 = f32[128,256]{1,0:T(8,128)S(1)} collective-permute-done((f32[128,256]{1,0:T(8,128)S(1)}, f32[128,256]{1,0:T(8,128)S(1)}, u32[]{:S(2)}, u32[]{:S(2)}) %collective-permute-start.5) | collective-permute-done | bytes 131104 | tf_op jit(solution)/shard_map/ppermute | solution.py:14
  57.0 0.8 copy.15
  57.9 63.5 %reduce-scatter.4.cloned.1.call-done = f32[32,256]{1,0:T(8,128)} async-done(((f32[256,256]{1,0:T(8,128)}), f32[32,256]{1,0:T(8,128)}) %reduce-scatter.4.cloned.1.call-update) | async-done | bytes 32784
  121.4 1.4 %bitcast_multiply_fusion.2 = f32[256,32]{0,1:T(8,128)} fusion(f32[32,256]{1,0:T(8,128)} %reduce-scatter.4.cloned.1.call-done), kind=kLoop, calls=%fused_computation.71 | loop fusion | flops 8192 | bytes 65536 | tf_op jit(solution)/shard_map/mul | solution.py:80
  (43 shorter events, 1.9 us)
Async XLA Ops:
  6.5 3.2 %copy-start.2 = (s32[256,8]{0,1:T(8,128)S(1)}, s32[256,8]{0,1:T(8,128)}, u32[]{:S(2)}) copy-start(s32[256,8]{0,1:T(8,128)} %param.11) | copy-start | bytes 24580
  6.5 3.7 %copy-start.1 = (s32[256,1024]{1,0:T(8,128)S(1)}, s32[256,1024]{1,0:T(8,128)}, u32[]{:S(2)}) copy-start(s32[256,1024]{1,0:T(8,128)} %param.10) | copy-start | bytes 3145732
  6.5 114.8 %reduce-scatter.4.cloned.1.call-start = ((), (), s32[]{:S(2)}) async-start(), calls=%async_computation.1 | async-start | bytes 294912
  10.6 2.2 %copy-start = (s32[1024,1024]{1,0:T(8,128)S(1)}, s32[1024,1024]{1,0:T(8,128)}, u32[]{:S(2)}) copy-start(s32[1024,1024]{1,0:T(8,128)} %param.7) | copy-start | bytes 12582916
  13.8 12.0 %collective-permute-start = (bf16[128,1024]{1,0:T(8,128)(2,1)S(1)}, bf16[128,1024]{1,0:T(8,128)(2,1)S(1)}, u32[]{:S(2)}, u32[]{:S(2)}) collective-permute-start(bf16[128,1024]{1,0:T(8,128)(2,1)S(1)} %copy.28), channel_id=1, source_target_pairs={{3,0},{0,1},{1,2},{2,3},{7,4},{4,5},{5,6},{6,7},{11,8},{8,9},{9,10... | collective-permute-start | bytes 786440 | tf_op jit(solution)/shard_map/while/body/eval_jaxpr/ppermute | solution.py:14
  16.5 5.7 %collective-permute-start.1 = (f32[128,256]{1,0:T(8,128)S(1)}, f32[128,256]{1,0:T(8,128)S(1)}, u32[]{:S(2)}, u32[]{:S(2)}) collective-permute-start(f32[128,256]{1,0:T(8,128)S(1)} %convolution_add_fusion.6), channel_id=1, source_target_pairs={{3,0},{0,1},{1,2},{2,3},{7,4},{4,5},{5,6},{6,7},{11,8},{8,9},{9,10... | collective-permute-start | bytes 393224 | tf_op jit(solution)/shard_map/while/body/eval_jaxpr/ppermute | solution.py:14
  19.2 6.6 %collective-permute-start.2 = (bf16[128,1024]{1,0:T(8,128)(2,1)S(1)}, bf16[128,1024]{1,0:T(8,128)(2,1)S(1)}, u32[]{:S(2)}, u32[]{:S(2)}) collective-permute-start(bf16[128,1024]{1,0:T(8,128)(2,1)S(1)} %copy.30), channel_id=1, source_target_pairs={{1,0},{2,1},{3,2},{0,3},{5,4},{6,5},{7,6},{4,7},{9,8},{10,9},{11,1... | collective-permute-start | bytes 786440 | tf_op jit(solution)/shard_map/while/body/eval_jaxpr/ppermute | solution.py:14
  22.2 3.6 %collective-permute-start.3 = (f32[128,256]{1,0:T(8,128)}, f32[128,256]{1,0:T(8,128)S(1)}, u32[]{:S(2)}, u32[]{:S(2)}) collective-permute-start(f32[128,256]{1,0:T(8,128)} %convolution_add_fusion.7), channel_id=1, source_target_pairs={{1,0},{2,1},{3,2},{0,3},{5,4},{6,5},{7,6},{4,7},{9,8},{10,9},{11,1... | collective-permute-start | bytes 393224 | tf_op jit(solution)/shard_map/while/body/eval_jaxpr/ppermute | solution.py:14
  25.8 11.4 %collective-permute-start = (bf16[128,1024]{1,0:T(8,128)(2,1)S(1)}, bf16[128,1024]{1,0:T(8,128)(2,1)S(1)}, u32[]{:S(2)}, u32[]{:S(2)}) collective-permute-start(bf16[128,1024]{1,0:T(8,128)(2,1)S(1)} %copy.28), channel_id=1, source_target_pairs={{3,0},{0,1},{1,2},{2,3},{7,4},{4,5},{5,6},{6,7},{11,8},{8,9},{9,10... | collective-permute-start | bytes 786440 | tf_op jit(solution)/shard_map/while/body/eval_jaxpr/ppermute | solution.py:14
  29.6 4.8 %collective-permute-start.1 = (f32[128,256]{1,0:T(8,128)S(1)}, f32[128,256]{1,0:T(8,128)S(1)}, u32[]{:S(2)}, u32[]{:S(2)}) collective-permute-start(f32[128,256]{1,0:T(8,128)S(1)} %convolution_add_fusion.6), channel_id=1, source_target_pairs={{3,0},{0,1},{1,2},{2,3},{7,4},{4,5},{5,6},{6,7},{11,8},{8,9},{9,10... | collective-permute-start | bytes 393224 | tf_op jit(solution)/shard_map/while/body/eval_jaxpr/ppermute | solution.py:14
  29.7 7.5 %collective-permute-start.2 = (bf16[128,1024]{1,0:T(8,128)(2,1)S(1)}, bf16[128,1024]{1,0:T(8,128)(2,1)S(1)}, u32[]{:S(2)}, u32[]{:S(2)}) collective-permute-start(bf16[128,1024]{1,0:T(8,128)(2,1)S(1)} %copy.30), channel_id=1, source_target_pairs={{1,0},{2,1},{3,2},{0,3},{5,4},{6,5},{7,6},{4,7},{9,8},{10,9},{11,1... | collective-permute-start | bytes 786440 | tf_op jit(solution)/shard_map/while/body/eval_jaxpr/ppermute | solution.py:14
  34.4 2.9 %collective-permute-start.3 = (f32[128,256]{1,0:T(8,128)}, f32[128,256]{1,0:T(8,128)S(1)}, u32[]{:S(2)}, u32[]{:S(2)}) collective-permute-start(f32[128,256]{1,0:T(8,128)} %convolution_add_fusion.7), channel_id=1, source_target_pairs={{1,0},{2,1},{3,2},{0,3},{5,4},{6,5},{7,6},{4,7},{9,8},{10,9},{11,1... | collective-permute-start | bytes 393224 | tf_op jit(solution)/shard_map/while/body/eval_jaxpr/ppermute | solution.py:14
  37.3 10.8 %collective-permute-start = (bf16[128,1024]{1,0:T(8,128)(2,1)S(1)}, bf16[128,1024]{1,0:T(8,128)(2,1)S(1)}, u32[]{:S(2)}, u32[]{:S(2)}) collective-permute-start(bf16[128,1024]{1,0:T(8,128)(2,1)S(1)} %copy.28), channel_id=1, source_target_pairs={{3,0},{0,1},{1,2},{2,3},{7,4},{4,5},{5,6},{6,7},{11,8},{8,9},{9,10... | collective-permute-start | bytes 786440 | tf_op jit(solution)/shard_map/while/body/eval_jaxpr/ppermute | solution.py:14
  40.4 4.8 %collective-permute-start.1 = (f32[128,256]{1,0:T(8,128)S(1)}, f32[128,256]{1,0:T(8,128)S(1)}, u32[]{:S(2)}, u32[]{:S(2)}) collective-permute-start(f32[128,256]{1,0:T(8,128)S(1)} %convolution_add_fusion.6), channel_id=1, source_target_pairs={{3,0},{0,1},{1,2},{2,3},{7,4},{4,5},{5,6},{6,7},{11,8},{8,9},{9,10... | collective-permute-start | bytes 393224 | tf_op jit(solution)/shard_map/while/body/eval_jaxpr/ppermute | solution.py:14
  40.5 7.5 %collective-permute-start.2 = (bf16[128,1024]{1,0:T(8,128)(2,1)S(1)}, bf16[128,1024]{1,0:T(8,128)(2,1)S(1)}, u32[]{:S(2)}, u32[]{:S(2)}) collective-permute-start(bf16[128,1024]{1,0:T(8,128)(2,1)S(1)} %copy.30), channel_id=1, source_target_pairs={{1,0},{2,1},{3,2},{0,3},{5,4},{6,5},{7,6},{4,7},{9,8},{10,9},{11,1... | collective-permute-start | bytes 786440 | tf_op jit(solution)/shard_map/while/body/eval_jaxpr/ppermute | solution.py:14
  45.2 2.9 %collective-permute-start.3 = (f32[128,256]{1,0:T(8,128)}, f32[128,256]{1,0:T(8,128)S(1)}, u32[]{:S(2)}, u32[]{:S(2)}) collective-permute-start(f32[128,256]{1,0:T(8,128)} %convolution_add_fusion.7), channel_id=1, source_target_pairs={{1,0},{2,1},{3,2},{0,3},{5,4},{6,5},{7,6},{4,7},{9,8},{10,9},{11,1... | collective-permute-start | bytes 393224 | tf_op jit(solution)/shard_map/while/body/eval_jaxpr/ppermute | solution.py:14
  50.3 4.5 %collective-permute-start.4 = (f32[128,256]{1,0:T(8,128)S(1)}, f32[128,256]{1,0:T(8,128)S(1)}, u32[]{:S(2)}, u32[]{:S(2)}) collective-permute-start(f32[128,256]{1,0:T(8,128)S(1)} %convolution_add_fusion.3), channel_id=1, source_target_pairs={{3,0},{0,1},{1,2},{2,3},{7,4},{4,5},{5,6},{6,7},{11,8},{8,9},{9,10... | collective-permute-start | bytes 393224 | tf_op jit(solution)/shard_map/ppermute | solution.py:14
  54.1 2.9 %collective-permute-start.5 = (f32[128,256]{1,0:T(8,128)S(1)}, f32[128,256]{1,0:T(8,128)S(1)}, u32[]{:S(2)}, u32[]{:S(2)}) collective-permute-start(f32[128,256]{1,0:T(8,128)S(1)} %convolution_add_fusion.2), channel_id=1, source_target_pairs={{1,0},{2,1},{3,2},{0,3},{5,4},{6,5},{7,6},{4,7},{9,8},{10,9},{11,1... | collective-permute-start | bytes 393224 | tf_op jit(solution)/shard_map/ppermute | solution.py:14
Sparse Core Ops, SparseCore 0:
  58.0 63.3 reduce-scatter.3
where the time goes:
time: 130 us
  waiting for transfers between devices  75.3 us (58%)
  matrix products  18.9 us (15%)
  between operations  13.5 us (10%)
  starting transfers between devices  11.3 us (9%)
  other arithmetic  6.67 us (5%)
  local copies, waits for them, and re-layouts  3.83 us (3%)
    unnamed x2, waiting for transfers between devices  63.5 us
    dot_general x8, matrix products, kernel_block(): return jnp.dot(matern, rhs_values, preferred_element_type=jnp.float32)  18.9 us
    ppermute x14, waiting for transfers between devices, shifted(): return lax.ppermute(block, axis, route)  11.8 us
    ppermute x14, starting transfers between devices, shifted(): return lax.ppermute(block, axis, route)  11.3 us
  transfers between devices with their start and end apart: 15, of which 6 were waited for; matrix products, arithmetic and copies ran while one was open for 14% of the time, Pallas kernels for 0%

commit v1 on v0

v1 whole, which is shorter than its diff:
```python
import functools
import math

import jax
import jax.numpy as jnp
from jax import lax
from jax.experimental import pallas as pl
from jax.experimental.pallas import tpu as pltpu
from jax.sharding import PartitionSpec as P

kernel_rate = 20.0
lanes = 128
src_chunks = 4
hop_chunks = 4
slab = 256
smallest = 2.0**-40
MESH = pl.DeviceIdType.MESH


def row_slice(start, size):
    return pl.ds(pl.multiple_of(start, size), size)


def dequantize_rows(codes, exps, start, count, gain, dst):
    levels = exps[:, row_slice(start, count)]
    factor = jnp.where(
        levels == 0,
        gain * 2.0**-9,
        jnp.where(levels == 1, gain * 2.0**-8, jnp.where(levels == 2, gain * 2.0**-7, gain * 2.0**-6)),
    ).astype(jnp.float32)
    factor = jnp.transpose(factor)
    blocks = exps.shape[0]
    width = codes.shape[1] // blocks
    total = None
    for j in range(blocks):
        columns = slice(j * width, (j + 1) * width)
        points = codes[row_slice(start, count), columns].astype(jnp.float32) * factor[:, j : j + 1]
        dst[row_slice(start, count), columns] = points.astype(jnp.bfloat16)
        total = points * points if total is None else total + points * points
    return total


def square_rows(points_ref, start, count):
    total = None
    for j in range(points_ref.shape[1] // lanes):
        points = points_ref[row_slice(start, count), j * lanes : (j + 1) * lanes].astype(jnp.float32)
        total = points * points if total is None else total + points * points
    return total


def kernel(
    ng, nb, sc_hbm, se_hbm, sg_hbm, tc_hbm, te_hbm, out_ref,
    sc, se, sg, tc, te, src, ssq, tgt, tsq, rhs, mat, acc,
    plane_send, plane_recv, hop_send, hop_recv, total,
    load_sem, core_send_sem, core_recv_sem, x_send_sem, x_recv_sem, f_send_sem, f_recv_sem,
    p_send_sem, p_recv_sem, h_send_sem, h_recv_sem,
):
    g = lax.axis_index("grp")
    b = lax.axis_index("blk")
    hs = nb // 2
    h, c = b // 2, lax.rem(b, 2)
    rows, width = sc.shape
    trows = tc.shape[0]
    rhs_count = sg.shape[1]
    part = rhs_count // ng
    half = trows // 2
    chunk = half // hop_chunks
    src_chunk = rows // src_chunks

    partner = (g, b + 1 - 2 * c)
    peers = [(g, lax.rem(h + j, hs) * 2 + c) for j in range(1, hs)]
    owners = [(g, lax.rem(h - j + hs, hs) * 2 + c) for j in range(1, hs)]
    plane = [(lax.rem(g + i, ng), b) for i in range(1, ng)]
    low, high = lax.rem(g, 2), lax.rem(g // 2, 2)
    side = lax.rem(low + high, 2)
    forward_to = [(g + 1 - 2 * low, b), (g + 2 - 4 * high, b)]

    load_te = pltpu.make_async_copy(te_hbm, te, load_sem.at[0])
    load_te.start()
    load_tc = pltpu.make_async_copy(tc_hbm, tc, load_sem.at[1])
    load_tc.start()
    load_se = pltpu.make_async_copy(se_hbm, se, load_sem.at[2])
    load_se.start()
    load_sc = []
    for k in range(src_chunks):
        piece = pl.ds(k * src_chunk, src_chunk)
        load_sc.append(pltpu.make_async_copy(sc_hbm.at[piece], sc.at[piece], load_sem.at[4 + k]))
        load_sc[-1].start()
    load_sg = pltpu.make_async_copy(sg_hbm, sg, load_sem.at[3])
    load_sg.start()

    barrier = pltpu.get_barrier_semaphore()
    greeted = [partner] + peers + plane
    for device in greeted:
        pl.semaphore_signal(barrier, inc=1, device_id=device, device_id_type=MESH)

    def own_targets(part_index):
        start = part_index * half
        squares = dequantize_rows(tc, te, start, half, -2.0, tgt.at[0])
        tsq[0, pl.ds(part_index, 1), :] = 0.25 * jnp.sum(jnp.transpose(squares), axis=0, keepdims=True)

    load_te.wait()
    load_tc.wait()
    own_targets(side)
    pl.semaphore_wait(barrier, len(greeted))

    def hop_rows(which, q):
        return row_slice(which * half + q * chunk, chunk)

    def x_copy(j, q):
        piece = hop_rows(side, q)
        return pltpu.make_async_remote_copy(
            src_ref=tgt.at[0, piece], dst_ref=tgt.at[j, piece],
            send_sem=x_send_sem.at[j - 1, q], recv_sem=x_recv_sem.at[j - 1, q],
            device_id=peers[j - 1], device_id_type=MESH,
        )

    def f_copy(j, q, which):
        piece = hop_rows(which, q)
        return pltpu.make_async_remote_copy(
            src_ref=tgt.at[j, piece], dst_ref=tgt.at[j, piece],
            send_sem=f_send_sem.at[j - 1, q], recv_sem=f_recv_sem.at[j - 1, q],
            device_id=forward_to[q % 2], device_id_type=MESH,
        )

    for q in range(hop_chunks):
        for j in range(1, hs):
            x_copy(j, q).start()
    own_targets(1 - side)

    def forward(q):
        for j in range(1, hs):
            x_copy(j, q).wait_recv()
            f_copy(j, q, side).start()

    def src_copy(k):
        return pltpu.make_async_remote_copy(
            src_ref=src.at[0, pl.ds(k * src_chunk, src_chunk)],
            dst_ref=src.at[1, pl.ds(k * src_chunk, src_chunk)],
            send_sem=core_send_sem.at[k], recv_sem=core_recv_sem.at[k],
            device_id=partner, device_id_type=MESH,
        )

    rhs_copy = pltpu.make_async_remote_copy(
        src_ref=rhs.at[0], dst_ref=rhs.at[1],
        send_sem=core_send_sem.at[src_chunks], recv_sem=core_recv_sem.at[src_chunks],
        device_id=partner, device_id_type=MESH,
    )

    def keep_source_squares(slot, start, squares):
        summed = jnp.sum(squares, axis=1, keepdims=True)
        ssq[slot, row_slice(start, lanes), :] = jnp.broadcast_to(summed, (lanes, lanes))

    load_se.wait()
    for k in range(src_chunks):
        load_sc[k].wait()

        @pl.loop(0, src_chunk // lanes)
        def _(i):
            start = k * src_chunk + i * lanes
            keep_source_squares(0, start, dequantize_rows(sc, se, start, lanes, 1.0, src.at[0]))

        src_copy(k).start()

    load_sg.wait()

    @pl.loop(0, rows // lanes)
    def _(i):
        signs = sg[row_slice(i * lanes, lanes), :].astype(jnp.float32)
        values = jnp.transpose(2.0 * signs - 1.0)
        rhs[0, :, row_slice(i * lanes, lanes)] = values.astype(jnp.bfloat16)

    rhs_copy.start()
    forward(0)

    rate = kernel_rate / math.sqrt(width)

    def matern_slabs(slot, j):
        target_sq = jnp.concatenate([tsq[j, 0:1, :], tsq[j, 1:2, :]], axis=1)

        @pl.loop(0, rows // slab)
        def _(i):
            piece = row_slice(i * slab, slab)
            inner = lax.dot_general(
                src[slot, piece, :], tgt[j], (((1,), (1,)), ((), ())),
                preferred_element_type=jnp.float32,
            )
            source_sq = ssq[slot, piece, :]
            source_sq = jnp.concatenate([source_sq] * (trows // lanes), axis=1)
            squared = jnp.maximum((source_sq + target_sq) + inner, smallest)
            distance = squared * lax.rsqrt(squared)
            decay = jnp.exp2(distance * (-rate * math.log2(math.e)))
            growth = 1.0 + distance * (rate + distance * (rate * rate / 3.0))
            mat[slot, piece, :] = (growth * decay).astype(jnp.bfloat16)

    def plane_copies(j):
        copies = []
        for i in range(1, ng):
            copies.append(pltpu.make_async_remote_copy(
                src_ref=plane_send.at[j, row_slice(plane[i - 1][0] * part, part)],
                dst_ref=plane_recv.at[j, i - 1],
                send_sem=p_send_sem.at[j], recv_sem=p_recv_sem.at[j],
                device_id=plane[i - 1], device_id_type=MESH,
            ))
        return copies

    def multiply_and_send(j):
        sums = jnp.dot(rhs[0], mat[0], preferred_element_type=jnp.float32)
        sums = sums + jnp.dot(rhs[1], mat[1], preferred_element_type=jnp.float32)
        acc[...] = sums
        plane_send[j] = sums.astype(jnp.bfloat16)
        for copy in plane_copies(j):
            copy.start()
        total[j] = acc[row_slice(g * part, part), :]

    def plane_total(j):
        pltpu.make_async_copy(plane_recv.at[j], plane_recv.at[j], p_recv_sem.at[j]).wait()
        sums = total[j]
        for i in range(ng - 1):
            sums = sums + plane_recv[j, i].astype(jnp.float32)
        return sums

    matern_slabs(0, 0)
    forward(1)
    for k in range(src_chunks):
        src_copy(k).wait_recv()

    @pl.loop(0, rows // lanes)
    def _(i):
        keep_source_squares(1, i * lanes, square_rows(src.at[1], i * lanes, lanes))

    matern_slabs(1, 0)
    forward(2)
    rhs_copy.wait_recv()
    multiply_and_send(0)
    for q in range(3, hop_chunks):
        forward(q)

    def hop_copy(j):
        return pltpu.make_async_remote_copy(
            src_ref=hop_send.at[j - 1], dst_ref=hop_recv.at[j - 1],
            send_sem=h_send_sem.at[j - 1], recv_sem=h_recv_sem.at[j - 1],
            device_id=owners[j - 1], device_id_type=MESH,
        )

    def target_squares(j, which):
        squares = square_rows(tgt.at[j], which * half, half)
        tsq[j, pl.ds(which, 1), :] = 0.25 * jnp.sum(jnp.transpose(squares), axis=0, keepdims=True)

    for j in range(1, hs):
        target_squares(j, side)
        for q in range(hop_chunks):
            f_copy(j, q, 1 - side).wait_recv()
        target_squares(j, 1 - side)
        matern_slabs(0, j)
        matern_slabs(1, j)
        multiply_and_send(j)

    result = plane_total(0)
    for j in range(1, hs):
        hop_send[j - 1] = plane_total(j)
        hop_copy(j).start()
    for j in range(1, hs):
        hop_copy(j).wait_recv()
        result = result + hop_recv[j - 1]
    out_ref[...] = result * (4.0 / math.sqrt(rows * ng * nb))

    for j in range(1, hs):
        for q in range(hop_chunks):
            x_copy(j, q).wait_send()
            f_copy(j, q, side).wait_send()
        hop_copy(j).wait_send()
    for k in range(src_chunks):
        src_copy(k).wait_send()
    rhs_copy.wait_send()
    for j in range(hs):
        pltpu.make_async_copy(plane_recv.at[j], plane_recv.at[j], p_send_sem.at[j]).wait()


def per_device(src_codes, src_exps, signs, tgt_codes, tgt_exps):
    ng, nb = lax.axis_size("grp"), lax.axis_size("blk")
    hs = nb // 2
    rows, width = src_codes.shape
    trows = tgt_codes.shape[0]
    rhs_count = signs.shape[1]
    blocks = src_exps.shape[1]
    part = rhs_count // ng
    f32, bf16, i32 = jnp.float32, jnp.bfloat16, jnp.int32
    dma = pltpu.SemaphoreType.DMA
    out = pl.pallas_call(
        functools.partial(kernel, ng, nb),
        out_shape=jax.ShapeDtypeStruct((part, trows), f32),
        in_specs=[pl.BlockSpec(memory_space=pl.ANY)] * 5,
        out_specs=pl.BlockSpec(memory_space=pltpu.VMEM),
        scratch_shapes=[
            pltpu.VMEM((rows, width), i32),
            pltpu.VMEM((blocks, rows), i32),
            pltpu.VMEM((rows, rhs_count), i32),
            pltpu.VMEM((trows, width), i32),
            pltpu.VMEM((blocks, trows), i32),
            pltpu.VMEM((2, rows, width), bf16),
            pltpu.VMEM((2, rows, lanes), f32),
            pltpu.VMEM((hs, trows, width), bf16),
            pltpu.VMEM((hs, 2, trows // 2), f32),
            pltpu.VMEM((2, rhs_count, rows), bf16),
            pltpu.VMEM((2, rows, trows), bf16),
            pltpu.VMEM((rhs_count, trows), f32),
            pltpu.VMEM((hs, rhs_count, trows), bf16),
            pltpu.VMEM((hs, ng - 1, part, trows), bf16),
            pltpu.VMEM((hs - 1, part, trows), f32),
            pltpu.VMEM((hs - 1, part, trows), f32),
            pltpu.VMEM((hs, part, trows), f32),
            dma((4 + src_chunks,)),
            dma((src_chunks + 1,)),
            dma((src_chunks + 1,)),
            dma((hs - 1, hop_chunks)),
            dma((hs - 1, hop_chunks)),
            dma((hs - 1, hop_chunks)),
            dma((hs - 1, hop_chunks)),
            dma((hs,)),
            dma((hs,)),
            dma((hs - 1,)),
            dma((hs - 1,)),
        ],
        compiler_params=pltpu.CompilerParams(
            collective_id=0, has_side_effects=True, vmem_limit_bytes=60 << 20
        ),
        name="matern_product",
    )(src_codes, src_exps.T, signs, tgt_codes, tgt_exps.T)
    return out.T


def solution(mesh):
    placed = (
        P(("grp", "blk"), None),
        P(("grp", "blk"), None),
        P(("grp", "blk"), None),
        P("blk", None),
        P("blk", None),
    )
    return jax.shard_map(
        per_device, mesh=mesh, in_specs=placed, out_specs=P("blk", "grp"), check_vma=False
    )
```

time: 130 us -> 32.6 us (0.25)
  waiting for transfers between devices: 75.3 us -> 0 us
  Pallas kernels: 0 us -> 31 us
  matrix products: 18.9 us -> 0 us
  between operations: 13.5 us -> 0.01 us
  starting transfers between devices: 11.3 us -> 0 us
  other arithmetic: 6.67 us -> 0 us
  local copies, waits for them, and re-layouts: 3.83 us -> 1.38 us
    unnamed x2 -> x0, waiting for transfers between devices: 63.5 us -> none
    pallas_call x0 -> x1, Pallas kernels: none -> 31 us  [per_device(): pl.pallas_call(functools.partial(kernel, ng, nb), out_shape=jax.ShapeDtyp...]
    dot_general x8 -> x0, matrix products: 18.9 us -> none  [kernel_block(): return jnp.dot(matern, rhs_values, preferred_element_type=jnp.float32)]
    ppermute x14 -> x0, waiting for transfers between devices: 11.8 us -> none  [shifted(): return lax.ppermute(block, axis, route)]
    ppermute x14 -> x0, starting transfers between devices: 11.3 us -> none  [shifted(): return lax.ppermute(block, axis, route)]
    convert_element_type x2 -> x0, other arithmetic: 2.49 us -> none  [the longest x1 2.14 us: per_device(): rhs_values = (2 * signs - 1).astype(jnp.bfloat16)]
    reduce_sum x9 -> x0, other arithmetic: 1.92 us -> none  [squares(): return jnp.sum(widened * widened, axis=1)]
    mul x2 -> x0, local copies, waits for them, and re-layouts: 1.47 us -> none  [dequantize(): codes.reshape(points, blocks, columns // blocks).astype(jnp.float32)]
  transfers between devices with their start and end apart: 15 -> 0, of which waited for: 6 -> 0; matrix products, arithmetic and copies ran while one was open for 14% -> 0% of each run, Pallas kernels for 0% -> 0%
where the time goes in v1:
time: 32.6 us; the launch traced here: 32.4 us
  Pallas kernels  31 us (95%)
  local copies, waits for them, and re-layouts  1.38 us (4%)
    pallas_call x1, Pallas kernels, per_device(): pl.pallas_call(functools.partial(kernel, ng, nb), out_shape=jax.ShapeDtyp...  31 us
    unnamed x1, local copies, waits for them, and re-layouts  1.38 us

profile of v1, /device:TPU:0, one launch (start us, length us, event | category | flops | bytes accessed | tf_op | source)
XLA Modules:
  0.0 32.4 jit_solution(16214123013356164361)
XLA Ops:
  0.0 31.0 %matern_product.1 = f32[32,256]{1,0:T(8,128)} custom-call(s32[1024,1024]{1,0:T(8,128)} %sc_hbm.1, s32[8,1024]{1,0:T(8,128)} %bitcast.4, s32[1024,256]{1,0:T(8,128)} %sg_hbm.1, s32[256,1024]{1,0:T(8,128)} %tc_hbm.1, s32[8,256]{1,0:T(8,128)} %bitcast.5), custom_call_target="tpu_custom_call" | custom-call | tf_op jit(solution)/shard_map/matern_product/pallas_call | solution.py:290
  31.0 1.4 %copy.7 = f32[256,32]{0,1:T(8,128)} copy(f32[256,32]{0,1:T(8,128)} %bitcast.3) | data formatting | bytes 65536

commit v2 on v1

--- a/solution.py
+++ b/solution.py
@@ -11,8 +11,8 @@
 kernel_rate = 20.0
 lanes = 128
 src_chunks = 4
-hop_chunks = 4
-slab = 256
+hop_chunks = 2
+slab = 512
 smallest = 2.0**-40
 MESH = pl.DeviceIdType.MESH
 
@@ -230,10 +230,9 @@
         keep_source_squares(1, i * lanes, square_rows(src.at[1], i * lanes, lanes))
 
     matern_slabs(1, 0)
-    forward(2)
     rhs_copy.wait_recv()
     multiply_and_send(0)
-    for q in range(3, hop_chunks):
+    for q in range(2, hop_chunks):
         forward(q)
 
     def hop_copy(j):

time: 32.6 us -> 29.2 us (0.90)
  Pallas kernels: 31 us -> 27.6 us
    pallas_call x1, Pallas kernels: 31 us -> 27.6 us  [per_device(): pl.pallas_call(functools.partial(kernel, ng, nb), out_shape=jax.ShapeDtyp...]
where the time goes in v2:
time: 29.2 us; the launch traced here: 29 us
  Pallas kernels  27.6 us (95%)
  local copies, waits for them, and re-layouts  1.38 us (5%)
    pallas_call x1, Pallas kernels, per_device(): pl.pallas_call(functools.partial(kernel, ng, nb), out_shape=jax.ShapeDtyp...  27.6 us
    unnamed x1, local copies, waits for them, and re-layouts  1.38 us

profile of v2, /device:TPU:0, one launch (start us, length us, event | category | flops | bytes accessed | tf_op | source)
XLA Modules:
  0.0 29.0 jit_solution(4287656351088971380)
XLA Ops:
  0.0 27.6 %matern_product.1 = f32[32,256]{1,0:T(8,128)} custom-call(s32[1024,1024]{1,0:T(8,128)} %sc_hbm.1, s32[8,1024]{1,0:T(8,128)} %bitcast.4, s32[1024,256]{1,0:T(8,128)} %sg_hbm.1, s32[256,1024]{1,0:T(8,128)} %tc_hbm.1, s32[8,256]{1,0:T(8,128)} %bitcast.5), custom_call_target="tpu_custom_call" | custom-call | tf_op jit(solution)/shard_map/matern_product/pallas_call | solution.py:289
  27.6 1.4 %copy.7 = f32[256,32]{0,1:T(8,128)} copy(f32[256,32]{0,1:T(8,128)} %bitcast.3) | data formatting | bytes 65536

commit v3 on v2

--- a/solution.py
+++ b/solution.py
@@ -51,9 +51,9 @@
 def kernel(
     ng, nb, sc_hbm, se_hbm, sg_hbm, tc_hbm, te_hbm, out_ref,
     sc, se, sg, tc, te, src, ssq, tgt, tsq, rhs, mat, acc,
-    plane_send, plane_recv, hop_send, hop_recv, total,
+    sum_send, sum_recv, total,
     load_sem, core_send_sem, core_recv_sem, x_send_sem, x_recv_sem, f_send_sem, f_recv_sem,
-    p_send_sem, p_recv_sem, h_send_sem, h_recv_sem,
+    s_send_sem, s_recv_sem,
 ):
     g = lax.axis_index("grp")
     b = lax.axis_index("blk")
@@ -69,8 +69,10 @@
 
     partner = (g, b + 1 - 2 * c)
     peers = [(g, lax.rem(h + j, hs) * 2 + c) for j in range(1, hs)]
-    owners = [(g, lax.rem(h - j + hs, hs) * 2 + c) for j in range(1, hs)]
-    plane = [(lax.rem(g + i, ng), b) for i in range(1, ng)]
+    takers = [
+        [(lax.rem(g + i, ng), lax.rem(h - j + hs, hs) * 2 + c) for i in range(1 if j == 0 else 0, ng)]
+        for j in range(hs)
+    ]
     low, high = lax.rem(g, 2), lax.rem(g // 2, 2)
     side = lax.rem(low + high, 2)
     forward_to = [(g + 1 - 2 * low, b), (g + 2 - 4 * high, b)]
@@ -90,7 +92,7 @@
     load_sg.start()
 
     barrier = pltpu.get_barrier_semaphore()
-    greeted = [partner] + peers + plane
+    greeted = [partner] + [device for group in takers for device in group]
     for device in greeted:
         pl.semaphore_signal(barrier, inc=1, device_id=device, device_id_type=MESH)
 
@@ -193,32 +195,31 @@
             growth = 1.0 + distance * (rate + distance * (rate * rate / 3.0))
             mat[slot, piece, :] = (growth * decay).astype(jnp.bfloat16)
 
-    def plane_copies(j):
+    def sum_copies(j):
         copies = []
-        for i in range(1, ng):
+        for i, taker in enumerate(takers[j]):
             copies.append(pltpu.make_async_remote_copy(
-                src_ref=plane_send.at[j, row_slice(plane[i - 1][0] * part, part)],
-                dst_ref=plane_recv.at[j, i - 1],
-                send_sem=p_send_sem.at[j], recv_sem=p_recv_sem.at[j],
-                device_id=plane[i - 1], device_id_type=MESH,
+                src_ref=sum_send.at[j, row_slice(taker[0] * part, part)],
+                dst_ref=sum_recv.at[j, i],
+                send_sem=s_send_sem.at[j], recv_sem=s_recv_sem.at[j],
+                device_id=taker, device_id_type=MESH,
             ))
         return copies
 
     def multiply_and_send(j):
         sums = jnp.dot(rhs[0], mat[0], preferred_element_type=jnp.float32)
         sums = sums + jnp.dot(rhs[1], mat[1], preferred_element_type=jnp.float32)
-        acc[...] = sums
-        plane_send[j] = sums.astype(jnp.bfloat16)
-        for copy in plane_copies(j):
+        sum_send[j] = sums.astype(jnp.bfloat16)
+        for copy in sum_copies(j):
             copy.start()
-        total[j] = acc[row_slice(g * part, part), :]
-
-    def plane_total(j):
-        pltpu.make_async_copy(plane_recv.at[j], plane_recv.at[j], p_recv_sem.at[j]).wait()
-        sums = total[j]
-        for i in range(ng - 1):
-            sums = sums + plane_recv[j, i].astype(jnp.float32)
-        return sums
+        if j == 0:
+            acc[...] = sums
+            total[...] = acc[row_slice(g * part, part), :]
+
+    def sums_bytes(j, sem):
+        count = len(takers[j])
+        arrived = sum_recv.at[j, pl.ds(0, count)]
+        return pltpu.make_async_copy(arrived, arrived, sem.at[j])
 
     matern_slabs(0, 0)
     forward(1)
@@ -234,13 +235,6 @@
     multiply_and_send(0)
     for q in range(2, hop_chunks):
         forward(q)
-
-    def hop_copy(j):
-        return pltpu.make_async_remote_copy(
-            src_ref=hop_send.at[j - 1], dst_ref=hop_recv.at[j - 1],
-            send_sem=h_send_sem.at[j - 1], recv_sem=h_recv_sem.at[j - 1],
-            device_id=owners[j - 1], device_id_type=MESH,
-        )
 
     def target_squares(j, which):
         squares = square_rows(tgt.at[j], which * half, half)
@@ -255,25 +249,22 @@
         matern_slabs(1, j)
         multiply_and_send(j)
 
-    result = plane_total(0)
-    for j in range(1, hs):
-        hop_send[j - 1] = plane_total(j)
-        hop_copy(j).start()
-    for j in range(1, hs):
-        hop_copy(j).wait_recv()
-        result = result + hop_recv[j - 1]
+    result = total[...]
+    for j in range(hs):
+        sums_bytes(j, s_recv_sem).wait()
+        for i in range(len(takers[j])):
+            result = result + sum_recv[j, i].astype(jnp.float32)
     out_ref[...] = result * (4.0 / math.sqrt(rows * ng * nb))
 
     for j in range(1, hs):
         for q in range(hop_chunks):
             x_copy(j, q).wait_send()
             f_copy(j, q, side).wait_send()
-        hop_copy(j).wait_send()
     for k in range(src_chunks):
         src_copy(k).wait_send()
     rhs_copy.wait_send()
     for j in range(hs):
-        pltpu.make_async_copy(plane_recv.at[j], plane_recv.at[j], p_send_sem.at[j]).wait()
+        sums_bytes(j, s_send_sem).wait()
 
 
 def per_device(src_codes, src_exps, signs, tgt_codes, tgt_exps):
@@ -305,10 +296,8 @@
             pltpu.VMEM((2, rows, trows), bf16),
             pltpu.VMEM((rhs_count, trows), f32),
             pltpu.VMEM((hs, rhs_count, trows), bf16),
-            pltpu.VMEM((hs, ng - 1, part, trows), bf16),
-            pltpu.VMEM((hs - 1, part, trows), f32),
-            pltpu.VMEM((hs - 1, part, trows), f32),
-            pltpu.VMEM((hs, part, trows), f32),
+            pltpu.VMEM((hs, ng, part, trows), bf16),
+            pltpu.VMEM((part, trows), f32),
             dma((4 + src_chunks,)),
             dma((src_chunks + 1,)),
             dma((src_chunks + 1,)),
@@ -318,8 +307,6 @@
             dma((hs - 1, hop_chunks)),
             dma((hs,)),
             dma((hs,)),
-            dma((hs - 1,)),
-            dma((hs - 1,)),
         ],
         compiler_params=pltpu.CompilerParams(
             collective_id=0, has_side_effects=True, vmem_limit_bytes=60 << 20

time: 29.2 us -> 27.6 us (0.945)
  Pallas kernels: 27.6 us -> 26 us
    pallas_call x1, Pallas kernels: 27.6 us -> 26 us  [per_device(): pl.pallas_call(functools.partial(kernel, ng, nb), out_shape=jax.ShapeDtyp...]
where the time goes in v3:
time: 27.6 us; the launch traced here: 27.4 us
  Pallas kernels  26 us (94%)
  local copies, waits for them, and re-layouts  1.38 us (5%)
    pallas_call x1, Pallas kernels, per_device(): pl.pallas_call(functools.partial(kernel, ng, nb), out_shape=jax.ShapeDtyp...  26 us
    unnamed x1, local copies, waits for them, and re-layouts  1.38 us

profile of v3, /device:TPU:0, one launch (start us, length us, event | category | flops | bytes accessed | tf_op | source)
XLA Modules:
  0.0 27.4 jit_solution(4369592207294659146)
XLA Ops:
  0.0 26.0 %matern_product.1 = f32[32,256]{1,0:T(8,128)} custom-call(s32[1024,1024]{1,0:T(8,128)} %sc_hbm.1, s32[8,1024]{1,0:T(8,128)} %bitcast.4, s32[1024,256]{1,0:T(8,128)} %sg_hbm.1, s32[256,1024]{1,0:T(8,128)} %tc_hbm.1, s32[8,256]{1,0:T(8,128)} %bitcast.5), custom_call_target="tpu_custom_call" | custom-call | tf_op jit(solution)/shard_map/matern_product/pallas_call | solution.py:280
  26.1 1.4 %copy.7 = f32[256,32]{0,1:T(8,128)} copy(f32[256,32]{0,1:T(8,128)} %bitcast.3) | data formatting | bytes 65536
